TPU v7x, 32 devices: a whole 2x2x4 slice. The times are simulated.
32 devices in a mesh: farm: 2 (over x), body: 16 (over z, y, core).
Axes of the slice: x: 2, y: 2, z: 4, core: 2. Of those that a mesh axis runs over, the one named last changes fastest.
Arguments:
- incident: float32 [32, 2, 16, 768], P(('farm', 'body')), parts along dimension 0, may hold values from -6 to 6
- self_inverse: float32 [32, 2, 768, 768], P(('farm', 'body')), parts along dimension 0
- cross_blocks: float32 [32, 4, 2, 768, 768], P(('farm', 'body')), parts along dimension 0, may hold values from -0.046875 to 0.046875
- neighbours: int32 [32, 4], P(('farm', 'body')), parts along dimension 0, may hold values from -1 to 15, as said below
- panel_weight: float32 [32, 768], P(('farm', 'body')), parts along dimension 0, may hold values from -0.0546875 to 0.0546875
Outputs:
- sources: float32 [32, 2, 16, 768], P(('farm', 'body')), parts along dimension 0
- farm_force: float32 [2, 2, 16], P('farm'), parts along dimension 0
There are 2 independent parts, one for each index of `farm`. A program takes and returns all parts, laid end to end along the dimension named above; each array names one. Nothing has to cross between parts.
Inputs may be any that keep to these rules, and one draw needn't show every extreme that they name: `neighbours`: each row names distinct bodies other than its own, each within 8 positions of it around the closed loop of 16 bodies; some body names the body exactly 8 positions away.
All inputs are finite; a program needn't handle non-finite values.
Results may differ from a plain program's by a relative error of at most 0.0003.
Values sent between devices are 32-bit elements; how exact they have to be, the bound alone decides.
No kernel may reach another device: no remote copies, remote signals or barrier semaphores. Data moves between devices by JAX's collectives and lax.ppermute only.
A program may use at most 128 MiB of HBM per device.

v0:
```python
import jax
import jax.numpy as jnp
from jax import lax
from jax.sharding import PartitionSpec as P

ITERS = 6


def complex_apply(matrix, field):
    heads = field.shape[1]
    stacked = field.reshape(2 * heads, field.shape[2])
    dims = (((1,), (1,)), ((), ()))
    real_part = lax.dot_general(stacked, matrix[0], dims, precision=lax.Precision.HIGHEST)
    imag_part = lax.dot_general(stacked, matrix[1], dims, precision=lax.Precision.HIGHEST)
    return jnp.stack([real_part[:heads] - imag_part[heads:], real_part[heads:] + imag_part[:heads]])


def body(incident, self_inverse, cross_blocks, neighbours, panel_weight):
    field = incident[0]
    inverse_one = self_inverse[0]
    blocks = cross_blocks[0]
    index_row = neighbours[0]
    flag_row = index_row >= 0
    safe_row = jnp.where(flag_row, index_row, 0)
    slot_count = index_row.shape[0]
    sources = complex_apply(inverse_one, field)
    for sweep in range(ITERS):
        gathered = lax.all_gather(sources[None], "body", axis=0, tiled=True)
        nearby = jnp.take(gathered, safe_row, axis=0)
        total = field
        for slot in range(slot_count):
            total = total - jnp.where(
                flag_row[slot], complex_apply(blocks[slot], nearby[slot]), 0.0
            )
        sources = complex_apply(inverse_one, total)
    partial_force = jnp.einsum(
        "p,chp->ch", panel_weight[0], sources, precision=lax.Precision.HIGHEST
    )
    farm_force = lax.psum(partial_force, "body")
    return (sources[None], farm_force[None])


def solution(mesh):
    return jax.shard_map(
        body,
        mesh=mesh,
        in_specs=(
            P(("farm", "body"), None, None, None),
            P(("farm", "body"), None, None, None),
            P(("farm", "body"), None, None, None, None),
            P(("farm", "body"), None),
            P(("farm", "body"), None),
        ),
        out_specs=(P(("farm", "body"), None, None, None), P("farm", None, None)),
        check_vma=False,
    )
```

profile of v0, /device:TPU:0, one launch (start us, length us, event | category | flops | bytes accessed | tf_op | source)
XLA Modules:
  0.0 540.5 jit_solution(6577915295749978652)
XLA Ops:
  7.2 3.9 fusion.108
  16.7 41.6 %all-gather.13.cloned.1.call-done = f32[32,16,768]{2,1,0:T(8,128)} async-done(((f32[2,16,768]{2,1,0:T(8,128)}), f32[32,16,768]{2,1,0:T(8,128)}) %all-gather.13.cloned.1.call-update) | async-done | bytes 1572880 | tf_op jit(solution)/shard_map/all_gather | solution.py:28
  60.4 3.9 fusion.34
  68.2 3.9 fusion.10
  72.1 4.0 fusion.22
  76.1 3.9 fusion.58
  80.0 3.9 fusion.70
  83.9 3.9 fusion.82
  87.8 4.3 fusion.94
  99.9 38.7 %all-gather.15.cloned.1.call-done = f32[32,16,768]{2,1,0:T(8,128)} async-done(((f32[2,16,768]{2,1,0:T(8,128)}), f32[32,16,768]{2,1,0:T(8,128)}) %all-gather.15.cloned.1.call-update) | async-done | bytes 1572880 | tf_op jit(solution)/shard_map/all_gather | solution.py:28
  140.7 3.9 fusion.32
  144.6 3.9 fusion.44
  148.5 3.9 fusion.8
  152.4 4.0 fusion.20
  156.4 3.9 fusion.56
  160.3 3.9 fusion.68
  164.2 3.9 fusion.80
  168.1 4.0 fusion.92
  180.0 38.7 %all-gather.17.cloned.1.call-done = f32[32,16,768]{2,1,0:T(8,128)} async-done(((f32[2,16,768]{2,1,0:T(8,128)}), f32[32,16,768]{2,1,0:T(8,128)}) %all-gather.17.cloned.1.call-update) | async-done | bytes 1572880 | tf_op jit(solution)/shard_map/all_gather | solution.py:28
  220.8 3.9 fusion.30
  224.7 3.9 fusion.42
  228.6 3.9 fusion.6
  232.5 4.0 fusion.18
  236.5 3.9 fusion.54
  240.4 3.9 fusion.66
  244.3 3.9 fusion.78
  248.2 4.3 fusion.90
  260.4 38.7 %all-gather.19.cloned.1.call-done = f32[32,16,768]{2,1,0:T(8,128)} async-done(((f32[2,16,768]{2,1,0:T(8,128)}), f32[32,16,768]{2,1,0:T(8,128)}) %all-gather.19.cloned.1.call-update) | async-done | bytes 1572880 | tf_op jit(solution)/shard_map/all_gather | solution.py:28
  305.0 3.9 fusion.40
  312.8 4.0 fusion.16
  316.8 3.9 fusion.52
  320.7 3.9 fusion.64
  324.7 3.9 fusion.76
  328.5 4.0 fusion.88
  340.5 38.7 %all-gather.21.cloned.1.call-done = f32[32,16,768]{2,1,0:T(8,128)} async-done(((f32[2,16,768]{2,1,0:T(8,128)}), f32[32,16,768]{2,1,0:T(8,128)}) %all-gather.21.cloned.1.call-update) | async-done | bytes 1572880 | tf_op jit(solution)/shard_map/all_gather | solution.py:28
  385.2 3.9 fusion.38
  392.9 4.0 fusion.14
  397.0 3.9 fusion.50
  400.8 3.9 fusion.62
  404.8 3.9 fusion.74
  408.7 4.3 fusion.86
  420.8 38.7 %all-gather.23.cloned.1.call-done = f32[32,16,768]{2,1,0:T(8,128)} async-done(((f32[2,16,768]{2,1,0:T(8,128)}), f32[32,16,768]{2,1,0:T(8,128)}) %all-gather.23.cloned.1.call-update) | async-done | bytes 1572880 | tf_op jit(solution)/shard_map/all_gather | solution.py:28
  465.5 3.9 fusion.36
  473.3 4.0 fusion.12
  477.3 4.0 fusion.48
  481.4 3.9 fusion.60
  485.3 3.9 fusion.72
  501.3 32.1 %psum.7 = f32[1,2,16]{2,1,0:T(2,128)} all-reduce(f32[1,2,16]{2,1,0:T(2,128)S(1)} %bitcast.457), channel_id=1, replica_groups=mesh['farm'=2,'body'=16] {'body'}, use_global_device_ids=true, to_apply=%region_0.2 | all-reduce | flops 32 | bytes 256 | tf_op jit(solution)/shard_map/psum | solution.py:39
  (133 shorter events, 96.2 us)
Async XLA Ops:
  7.2 493.7 %copy-start = (f32[1,768]{1,0:T(1,128)S(1)}, f32[1,768]{1,0:T(1,128)}, u32[]{:S(2)}) copy-start(f32[1,768]{1,0:T(1,128)} %param.11) | copy-start | bytes 9220
  7.2 4.0 copy-start.1
  7.2 51.1 %all-gather.13.cloned.1.call-start = ((), (), s32[]{:S(2)}) async-start(), calls=%async_computation | async-start | bytes 1671168 | tf_op jit(solution)/shard_map/all_gather | solution.py:28
  7.2 8.8 %copy-start.2 = (s32[1,4]{1,0:T(1,128)S(1)}, s32[1,4]{1,0:T(1,128)}, u32[]{:S(2)}) copy-start(s32[1,4]{1,0:T(1,128)} %param.10) | copy-start | bytes 52
  15.8 122.8 %all-gather.15.cloned.1.call-start = ((), (), s32[]{:S(2)}) async-start(), calls=%async_computation.1 | async-start | bytes 1671168 | tf_op jit(solution)/shard_map/all_gather | solution.py:28
  72.0 22.6 %slice-start = ((s8[4718592]{0:T(1024)(128)(4,1)}), s8[4194304]{0:T(1024)(128)(4,1)S(1)}, s32[]{:S(2)}) async-start(s8[4718592]{0:T(1024)(128)(4,1)} %bitcast.377), calls=%async_computation.6 | async-start | bytes 8388608
  80.0 14.7 %slice-start.1 = ((s8[4718592]{0:T(1024)(128)(4,1)}), s8[524288]{0:T(1024)(128)(4,1)S(1)}, s32[]{:S(2)}) async-start(s8[4718592]{0:T(1024)(128)(4,1)} %bitcast.377), calls=%async_computation.7 | async-start | bytes 1048576
  99.9 118.8 %all-gather.17.cloned.1.call-start = ((), (), s32[]{:S(2)}) async-start(), calls=%async_computation.2 | async-start | bytes 1671168 | tf_op jit(solution)/shard_map/all_gather | solution.py:28
  152.4 22.4 %slice-start.2 = ((s8[4718592]{0:T(1024)(128)(4,1)}), s8[4194304]{0:T(1024)(128)(4,1)S(1)}, s32[]{:S(2)}) async-start(s8[4718592]{0:T(1024)(128)(4,1)} %bitcast.379), calls=%async_computation.8 | async-start | bytes 8388608
  160.3 14.5 %slice-start.3 = ((s8[4718592]{0:T(1024)(128)(4,1)}), s8[524288]{0:T(1024)(128)(4,1)S(1)}, s32[]{:S(2)}) async-start(s8[4718592]{0:T(1024)(128)(4,1)} %bitcast.379), calls=%async_computation.9 | async-start | bytes 1048576
  180.0 119.1 %all-gather.19.cloned.1.call-start = ((), (), s32[]{:S(2)}) async-start(), calls=%async_computation.3 | async-start | bytes 1671168 | tf_op jit(solution)/shard_map/all_gather | solution.py:28
  232.5 22.6 %slice-start.4 = ((s8[4718592]{0:T(1024)(128)(4,1)}), s8[4194304]{0:T(1024)(128)(4,1)S(1)}, s32[]{:S(2)}) async-start(s8[4718592]{0:T(1024)(128)(4,1)} %bitcast.381), calls=%async_computation.10 | async-start | bytes 8388608
  240.4 14.7 %slice-start.5 = ((s8[4718592]{0:T(1024)(128)(4,1)}), s8[524288]{0:T(1024)(128)(4,1)S(1)}, s32[]{:S(2)}) async-start(s8[4718592]{0:T(1024)(128)(4,1)} %bitcast.381), calls=%async_computation.11 | async-start | bytes 1048576
  260.3 118.8 %all-gather.21.cloned.1.call-start = ((), (), s32[]{:S(2)}) async-start(), calls=%async_computation.4 | async-start | bytes 1671168 | tf_op jit(solution)/shard_map/all_gather | solution.py:28
  312.8 22.4 %slice-start.6 = ((s8[4718592]{0:T(1024)(128)(4,1)}), s8[4194304]{0:T(1024)(128)(4,1)S(1)}, s32[]{:S(2)}) async-start(s8[4718592]{0:T(1024)(128)(4,1)} %bitcast.383), calls=%async_computation.12 | async-start | bytes 8388608
  320.7 14.5 %slice-start.7 = ((s8[4718592]{0:T(1024)(128)(4,1)}), s8[524288]{0:T(1024)(128)(4,1)S(1)}, s32[]{:S(2)}) async-start(s8[4718592]{0:T(1024)(128)(4,1)} %bitcast.383), calls=%async_computation.13 | async-start | bytes 1048576
  340.4 119.1 %all-gather.23.cloned.1.call-start = ((), (), s32[]{:S(2)}) async-start(), calls=%async_computation.5 | async-start | bytes 1671168 | tf_op jit(solution)/shard_map/all_gather | solution.py:28
  392.9 22.6 %slice-start.8 = ((s8[4718592]{0:T(1024)(128)(4,1)}), s8[4194304]{0:T(1024)(128)(4,1)S(1)}, s32[]{:S(2)}) async-start(s8[4718592]{0:T(1024)(128)(4,1)} %bitcast.385), calls=%async_computation.14 | async-start | bytes 8388608
  400.8 14.7 %slice-start.9 = ((s8[4718592]{0:T(1024)(128)(4,1)}), s8[524288]{0:T(1024)(128)(4,1)S(1)}, s32[]{:S(2)}) async-start(s8[4718592]{0:T(1024)(128)(4,1)} %bitcast.385), calls=%async_computation.15 | async-start | bytes 1048576
  473.2 22.4 %slice-start.10 = ((s8[4718592]{0:T(1024)(128)(4,1)}), s8[4194304]{0:T(1024)(128)(4,1)S(1)}, s32[]{:S(2)}) async-start(s8[4718592]{0:T(1024)(128)(4,1)} %bitcast.387), calls=%async_computation.16 | async-start | bytes 8388608
  481.3 14.3 %slice-start.11 = ((s8[4718592]{0:T(1024)(128)(4,1)}), s8[524288]{0:T(1024)(128)(4,1)S(1)}, s32[]{:S(2)}) async-start(s8[4718592]{0:T(1024)(128)(4,1)} %bitcast.387), calls=%async_computation.17 | async-start | bytes 1048576
Sparse Core Ops, SparseCore 0:
  15.9 42.3 all-gather.12
  100.0 38.5 all-gather.14
  180.1 38.5 all-gather.16
  260.4 38.5 all-gather.18
  340.6 38.5 all-gather.20
  420.9 38.5 all-gather.22
where the time goes:
time: 551 us; the launch traced here: 540 us
  waiting for transfers between devices  235 us (43%)
  matrix products  224 us (41%)
  blocking collectives  32.1 us (6%)
  other arithmetic  20.8 us (4%)
  between operations  15.4 us (3%)
  local copies, waits for them, and re-layouts  12.8 us (2%)
    all_gather x6, waiting for transfers between devices, body(): gathered = lax.all_gather(sources[None], 'body', axis=0, tiled=True)  235 us
    dot_general x31, matrix products, complex_apply(): lax.dot_general(stacked, matrix[0], dims, precision=lax.Precision.HIGHEST)  113 us
    dot_general x31, matrix products, complex_apply(): lax.dot_general(stacked, matrix[1], dims, precision=lax.Precision.HIGHEST)  110 us
    psum x1, blocking collectives, body(): farm_force = lax.psum(partial_force, 'body')  32.1 us
    sub x6, other arithmetic, body(): total - jnp.where(flag_row[slot], complex_apply(blocks[slot], nearby[slot...  15.2 us
    gather x6, local copies, waits for them, and re-layouts, body(): nearby = jnp.take(gathered, safe_row, axis=0)  11.9 us
  transfers between devices with their start and end apart: 6, of which 6 were waited for; matrix products, arithmetic and copies ran while one was open for 0% of the time, Pallas kernels for 0%

commit v1 on v0

v1 whole, which is shorter than its diff:
```python
import functools

import jax
import jax.numpy as jnp
from jax import lax
from jax.experimental import pallas as pl
from jax.experimental.pallas import tpu as pltpu
from jax.sharding import PartitionSpec as P

ITERS = 6
NT = (((1,), (1,)), ((), ()))
TILE = 256


def split(x):
    hi = x.astype(jnp.bfloat16)
    lo = (x - hi.astype(jnp.float32)).astype(jnp.bfloat16)
    return hi, lo


def turn(x, heads):
    return jnp.concatenate([-x[heads:], x[:heads]], axis=0)


def put_field(lhs, slot, x, heads):
    hi, lo = split(x)
    hi, lo = hi.astype(jnp.float32), lo.astype(jnp.float32)
    lhs[2 * slot] = jnp.concatenate([hi, lo], axis=0).astype(jnp.bfloat16)
    lhs[2 * slot + 1] = jnp.concatenate(
        [turn(hi, heads), turn(lo, heads)], axis=0
    ).astype(jnp.bfloat16)


def product(lhs, hi_ref, lo_ref, count, store):
    rows = lhs.shape[1] // 2
    panels = lhs.shape[2]
    for start in range(0, panels, TILE):
        part = slice(start, start + TILE)
        both, low = None, None
        for j in range(count):
            a = lax.dot_general(lhs[j], hi_ref[j, part, :], NT, preferred_element_type=jnp.float32)
            b = lax.dot_general(lhs[j, :rows], lo_ref[j, part, :], NT, preferred_element_type=jnp.float32)
            both = a if both is None else both + a
            low = b if low is None else low + b
        store(part, both[:rows] + both[rows:] + low)


def split_kernel(m_ref, hi_ref, lo_ref):
    hi, lo = split(m_ref[0])
    j = pl.program_id(0)
    hi_ref[j] = hi
    lo_ref[j] = lo


def split_matrices(m):
    count, rows, cols = m.shape
    whole = pl.BlockSpec(m.shape, lambda j: (0, 0, 0))
    out = jax.ShapeDtypeStruct(m.shape, jnp.bfloat16)
    return pl.pallas_call(
        split_kernel,
        grid=(count,),
        in_specs=[pl.BlockSpec((1, rows, cols), lambda j: (j, 0, 0))],
        out_specs=[pl.BlockSpec(memory_space=pltpu.VMEM)] * 2,
        out_shape=[out, out],
        compiler_params=pltpu.CompilerParams(vmem_limit_bytes=12 * 2**20),
    )(m)


def first_kernel(heads, field_ref, hi_ref, lo_ref, out_ref, lhs):
    put_field(lhs, 0, field_ref[...], heads)

    def store(part, value):
        out_ref[:, part] = value

    product(lhs, hi_ref, lo_ref, 2, store)


def sweep_kernel(heads, slots, count, which_ref, *refs):
    blocks = refs[:count]
    field_ref, chi, clo, ihi, ilo, out_ref, near, lhs, load, sem = refs[count:]
    for k in range(slots):
        for j in range(count):
            @pl.when(which_ref[k] == j)
            def _():
                pltpu.make_async_copy(blocks[j], near.at[k], sem.at[k]).start()
    for k in range(slots):
        @pl.when(which_ref[k] >= 0)
        def _():
            pltpu.make_async_copy(blocks[0], near.at[k], sem.at[k]).wait()
            put_field(lhs, k, near[k], heads)

        @pl.when(which_ref[k] < 0)
        def _():
            put_field(lhs, k, jnp.zeros(near.shape[1:], jnp.float32), heads)

    def store_load(part, value):
        load[:, part] = field_ref[:, part] - value

    product(lhs, chi, clo, 2 * slots, store_load)
    put_field(lhs, 0, load[...], heads)

    def store(part, value):
        out_ref[:, part] = value

    product(lhs, ihi, ilo, 2, store)


def body(count, incident, self_inverse, cross_blocks, neighbours, panel_weight):
    _, _, heads, panels = incident.shape
    slots = cross_blocks.shape[1]
    rows = 2 * heads
    field = incident.reshape(rows, panels)
    me = lax.axis_index("body")
    lines = count // 4

    def rel(index):
        dz = lax.rem(me // 4 - index // 4 + lines, lines)
        return dz * 4 + jnp.bitwise_xor(lax.rem(index, 4), lax.rem(me, 4))

    row = neighbours[0]
    which = jnp.where(row >= 0, rel(jnp.maximum(row, 0)), -1)
    vmem = pl.BlockSpec(memory_space=pltpu.VMEM)
    out = jax.ShapeDtypeStruct((rows, panels), jnp.float32)
    small = pltpu.CompilerParams(vmem_limit_bytes=12 * 2**20)
    ihi, ilo = split_matrices(self_inverse[0])
    chi, clo = split_matrices(cross_blocks[0].reshape(2 * slots, panels, panels))
    sources = pl.pallas_call(
        functools.partial(first_kernel, heads),
        in_specs=[vmem] * 3,
        out_specs=vmem,
        out_shape=out,
        scratch_shapes=[pltpu.VMEM((2, 2 * rows, panels), jnp.bfloat16)],
        compiler_params=small,
    )(field, ihi, ilo)
    sweep_call = pl.pallas_call(
        functools.partial(sweep_kernel, heads, slots, count),
        in_specs=[pl.BlockSpec(memory_space=pltpu.SMEM)]
        + [pl.BlockSpec(memory_space=pl.ANY)] * count
        + [vmem] * 5,
        out_specs=vmem,
        out_shape=out,
        scratch_shapes=[
            pltpu.VMEM((slots, rows, panels), jnp.float32),
            pltpu.VMEM((2 * slots, 2 * rows, panels), jnp.bfloat16),
            pltpu.VMEM((rows, panels), jnp.float32),
            pltpu.SemaphoreType.DMA((slots,)),
        ],
        compiler_params=small,
    )

    def move(x, pairs):
        return lax.ppermute(x, "body", pairs)

    z_pairs = [[(i, (i + 4 * d) % count) for i in range(count)] for d in range(lines)]
    y_pairs = [(i, i ^ 2) for i in range(count)]
    c_pairs = [(i, i ^ 1) for i in range(count)]
    for sweep in range(ITERS):
        blocks = [None] * count
        for d in range(lines):
            blocks[4 * d] = sources if d == 0 else move(sources, z_pairs[d])
        for d in range(lines):
            blocks[4 * d + 2] = move(blocks[4 * d], y_pairs)
        for d in range(lines):
            blocks[4 * d + 1] = move(blocks[4 * d], c_pairs)
        for d in range(lines):
            blocks[4 * d + 3] = move(blocks[4 * d + 2], c_pairs)
        sources = sweep_call(which, *blocks, field, chi, clo, ihi, ilo)
    partial_force = jnp.sum(
        sources.reshape(2, heads, panels) * panel_weight[0][None, None], axis=-1
    )
    farm_force = lax.psum(partial_force, "body")
    return (sources.reshape(1, 2, heads, panels), farm_force[None])


def solution(mesh):
    return jax.shard_map(
        functools.partial(body, mesh.shape["body"]),
        mesh=mesh,
        in_specs=(
            P(("farm", "body"), None, None, None),
            P(("farm", "body"), None, None, None),
            P(("farm", "body"), None, None, None, None),
            P(("farm", "body"), None),
            P(("farm", "body"), None),
        ),
        out_specs=(P(("farm", "body"), None, None, None), P("farm", None, None)),
        check_vma=False,
    )
```

time: 551 us -> 243 us (0.44); the launches traced: 540 us -> 242 us
  matrix products: 224 us -> 0 us
  waiting for transfers between devices: 235 us -> 54.3 us
  Pallas kernels: 0 us -> 70.8 us
  starting transfers between devices: 0.43 us -> 63 us
  other arithmetic: 20.8 us -> 1.04 us
  between operations: 15.4 us -> 0.94 us
  local copies, waits for them, and re-layouts: 12.8 us -> 20.2 us
    all_gather x6 -> x0, waiting for transfers between devices: 235 us -> none  [body(): gathered = lax.all_gather(sources[None], 'body', axis=0, tiled=True)]
    dot_general x63 -> x0, matrix products: 224 us -> none  [the longest x31 113 us: complex_apply(): lax.dot_general(stacked, matrix[0], dims, precision=lax.Precision.HIGHEST)]
    pallas_call x0 -> x9, Pallas kernels: none -> 70.8 us  [the longest x6 65.8 us: body(): sources = sweep_call(which, *blocks, field, chi, clo, ihi, ilo)]
    ppermute x0 -> x90, starting transfers between devices: none -> 63 us  [move(): return lax.ppermute(x, 'body', pairs)]
    ppermute x0 -> x90, waiting for transfers between devices: none -> 54.3 us  [move(): return lax.ppermute(x, 'body', pairs)]
    unnamed x30 -> x26, local copies, waits for them, and re-layouts: 0.11 us -> 20.1 us
    sub x6 -> x0, other arithmetic: 15.2 us -> none  [body(): total - jnp.where(flag_row[slot], complex_apply(blocks[slot], nearby[slot...]
    gather x6 -> x0, local copies, waits for them, and re-layouts: 11.9 us -> none  [body(): nearby = jnp.take(gathered, safe_row, axis=0)]
  transfers between devices with their start and end apart: 6 -> 90, of which waited for: 6 -> 39; matrix products, arithmetic and copies ran while one was open for 0% -> 0% of each run, Pallas kernels for 0% -> 1%
where the time goes in v1:
time: 243 us; the launch traced here: 242 us
  Pallas kernels  70.8 us (29%)
  starting transfers between devices  63 us (26%)
  waiting for transfers between devices  54.3 us (22%)
  blocking collectives  32.3 us (13%)
  local copies, waits for them, and re-layouts  20.2 us (8%)
    pallas_call x6, Pallas kernels, body(): sources = sweep_call(which, *blocks, field, chi, clo, ihi, ilo)  65.8 us
    ppermute x90, starting transfers between devices, move(): return lax.ppermute(x, 'body', pairs)  63 us
    ppermute x90, waiting for transfers between devices, move(): return lax.ppermute(x, 'body', pairs)  54.3 us
    psum x1, blocking collectives, body(): farm_force = lax.psum(partial_force, 'body')  32.3 us
    unnamed x26, local copies, waits for them, and re-layouts  20.1 us
  transfers between devices with their start and end apart: 90, of which 39 were waited for; matrix products, arithmetic and copies ran while one was open for 0% of the time, Pallas kernels for 1%

profile of v1, /device:TPU:0, one launch (start us, length us, event | category | flops | bytes accessed | tf_op | source)
XLA Modules:
  0.0 242.5 jit_solution(9338185016412827176)
XLA Ops:
  0.6 2.3 copy-done.10
  4.6 1.5 shard_map.69.refs_0_
  6.1 1.4 copy-done.4
  7.5 4.0 %collective-permute-start.7 = (f32[32,768]{1,0:T(8,128)S(1)}, f32[32,768]{1,0:T(8,128)S(1)}, u32[]{:S(2)}, u32[]{:S(2)}) collective-permute-start(f32[32,768]{1,0:T(8,128)S(1)} %shard_map.69.refs_0_), channel_id=1, source_target_pairs={{0,8},{1,9},{2,10},{3,11},{4,12},{5,13},{6,14},{7,15},{8,0},{9,1},... | collective-permute-start | bytes 294920 | tf_op jit(solution)/shard_map/ppermute | solution.py:152
  13.6 1.5 collective-permute-start.1
  15.1 2.8 %collective-permute-done.7.refs_8_ = f32[32,768]{1,0:T(8,128)S(1)} collective-permute-done((f32[32,768]{1,0:T(8,128)S(1)}, f32[32,768]{1,0:T(8,128)S(1)}, u32[]{:S(2)}, u32[]{:S(2)}) %collective-permute-start.7) | collective-permute-done | bytes 98336 | tf_op jit(solution)/shard_map/ppermute | solution.py:152
  17.9 1.7 collective-permute-start.9
  19.9 1.7 collective-permute-start.5
  26.3 6.4 %copy-done.7 = f32[1,4,2,768,768]{4,3,2,1,0:T(8,128)S(1)} copy-done((f32[1,4,2,768,768]{4,3,2,1,0:T(8,128)S(1)}, f32[1,4,2,768,768]{4,3,2,1,0:T(8,128)}, u32[]{:S(2)}) %copy-start.7) | copy-done | bytes 18874392
  32.6 2.8 %shard_map.70 = (bf16[8,768,768]{2,1,0:T(8,128)(2,1)S(1)}, bf16[8,768,768]{2,1,0:T(8,128)(2,1)S(1)}) custom-call(f32[8,768,768]{2,1,0:T(8,128)S(1)} %bitcast.16), custom_call_target="tpu_custom_call" | custom-call | tf_op jit(solution)/shard_map/pallas_call | solution.py:59
  35.6 10.9 %shard_map.71.refs_0_ = f32[32,768]{1,0:T(8,128)S(1)} custom-call(s32[4]{0:T(128)S(1)} %bitcast_select_fusion.1.which_ref, f32[32,768]{1,0:T(8,128)S(1)} %shard_map.69.refs_0_, f32[32,768]{1,0:T(8,128)S(1)} %collective-permute-done.refs_1_, f32[32,768]{1,0:T(8,128)S(1)} %collective-permute-done.1.refs_2_, f32[32,768]{1,0:T(8,128)S(1)} %collective-permute-done.2.refs_3_, ...), custom_call_target="tpu_custom_call" | custom-call | tf_op jit(solution)/shard_map/pallas_call | solution.py:167
  46.4 2.5 %collective-permute-start.18 = (f32[32,768]{1,0:T(8,128)S(1)}, f32[32,768]{1,0:T(8,128)S(1)}, u32[]{:S(2)}, u32[]{:S(2)}) collective-permute-start(f32[32,768]{1,0:T(8,128)S(1)} %shard_map.71.refs_0_), channel_id=1, source_target_pairs={{0,4},{1,5},{2,6},{3,7},{4,8},{5,9},{6,10},{7,11},{8,12},{9,13},{1... | collective-permute-start | bytes 294920 | tf_op jit(solution)/shard_map/ppermute | solution.py:152
  49.0 3.5 %collective-permute-start.22 = (f32[32,768]{1,0:T(8,128)S(1)}, f32[32,768]{1,0:T(8,128)S(1)}, u32[]{:S(2)}, u32[]{:S(2)}) collective-permute-start(f32[32,768]{1,0:T(8,128)S(1)} %shard_map.71.refs_0_), channel_id=1, source_target_pairs={{0,8},{1,9},{2,10},{3,11},{4,12},{5,13},{6,14},{7,15},{8,0},{9,1},... | collective-permute-start | bytes 294920 | tf_op jit(solution)/shard_map/ppermute | solution.py:152
  52.5 1.4 collective-permute-start.16
  53.9 1.7 collective-permute-done.18.refs_4_
  55.6 1.5 collective-permute-start.20
  57.1 2.4 collective-permute-done.22.refs_8_
  59.5 1.7 collective-permute-start.24
  62.1 2.8 %collective-permute-done.24.refs_10_ = f32[32,768]{1,0:T(8,128)S(1)} collective-permute-done((f32[32,768]{1,0:T(8,128)S(1)}, f32[32,768]{1,0:T(8,128)S(1)}, u32[]{:S(2)}, u32[]{:S(2)}) %collective-permute-start.24) | collective-permute-done | bytes 98336 | tf_op jit(solution)/shard_map/ppermute | solution.py:152
  68.1 10.8 %shard_map.72.refs_0_ = f32[32,768]{1,0:T(8,128)S(1)} custom-call(s32[4]{0:T(128)S(1)} %bitcast_select_fusion.1.which_ref, f32[32,768]{1,0:T(8,128)S(1)} %shard_map.71.refs_0_, f32[32,768]{1,0:T(8,128)S(1)} %collective-permute-done.15.refs_1_, f32[32,768]{1,0:T(8,128)S(1)} %collective-permute-done.16.refs_2_, f32[32,768]{1,0:T(8,128)S(1)} %collective-permute-done.17.refs_3_, ...), custom_call_target="tpu_custom_call" | custom-call | tf_op jit(solution)/shard_map/pallas_call | solution.py:167
  79.7 2.8 %collective-permute-start.37 = (f32[32,768]{1,0:T(8,128)S(1)}, f32[32,768]{1,0:T(8,128)S(1)}, u32[]{:S(2)}, u32[]{:S(2)}) collective-permute-start(f32[32,768]{1,0:T(8,128)S(1)} %shard_map.72.refs_0_), channel_id=1, source_target_pairs={{0,8},{1,9},{2,10},{3,11},{4,12},{5,13},{6,14},{7,15},{8,0},{9,1},... | collective-permute-start | bytes 294920 | tf_op jit(solution)/shard_map/ppermute | solution.py:152
  83.0 1.6 collective-permute-start.31
  84.7 2.1 collective-permute-done.33.refs_4_
  86.7 1.6 collective-permute-start.35
  88.4 1.8 collective-permute-done.37.refs_8_
  90.1 1.7 collective-permute-start.39
  92.8 2.1 collective-permute-done.39.refs_10_
  94.9 1.6 collective-permute-done.43.refs_14_
  98.2 10.8 %shard_map.73.refs_0_ = f32[32,768]{1,0:T(8,128)S(1)} custom-call(s32[4]{0:T(128)S(1)} %bitcast_select_fusion.1.which_ref, f32[32,768]{1,0:T(8,128)S(1)} %shard_map.72.refs_0_, f32[32,768]{1,0:T(8,128)S(1)} %collective-permute-done.30.refs_1_, f32[32,768]{1,0:T(8,128)S(1)} %collective-permute-done.31.refs_2_, f32[32,768]{1,0:T(8,128)S(1)} %collective-permute-done.32.refs_3_, ...), custom_call_target="tpu_custom_call" | custom-call | tf_op jit(solution)/shard_map/pallas_call | solution.py:167
  109.3 3.5 %collective-permute-start.52 = (f32[32,768]{1,0:T(8,128)S(1)}, f32[32,768]{1,0:T(8,128)S(1)}, u32[]{:S(2)}, u32[]{:S(2)}) collective-permute-start(f32[32,768]{1,0:T(8,128)S(1)} %shard_map.73.refs_0_), channel_id=1, source_target_pairs={{0,8},{1,9},{2,10},{3,11},{4,12},{5,13},{6,14},{7,15},{8,0},{9,1},... | collective-permute-start | bytes 294920 | tf_op jit(solution)/shard_map/ppermute | solution.py:152
  114.1 2.6 %collective-permute-done.48.refs_4_ = f32[32,768]{1,0:T(8,128)S(1)} collective-permute-done((f32[32,768]{1,0:T(8,128)S(1)}, f32[32,768]{1,0:T(8,128)S(1)}, u32[]{:S(2)}, u32[]{:S(2)}) %collective-permute-start.48) | collective-permute-done | bytes 98336 | tf_op jit(solution)/shard_map/ppermute | solution.py:152
  117.7 2.4 collective-permute-done.52.refs_8_
  122.7 2.8 %collective-permute-done.54.refs_10_ = f32[32,768]{1,0:T(8,128)S(1)} collective-permute-done((f32[32,768]{1,0:T(8,128)S(1)}, f32[32,768]{1,0:T(8,128)S(1)}, u32[]{:S(2)}, u32[]{:S(2)}) %collective-permute-start.54) | collective-permute-done | bytes 98336 | tf_op jit(solution)/shard_map/ppermute | solution.py:152
  128.4 10.8 %shard_map.74.refs_0_ = f32[32,768]{1,0:T(8,128)S(1)} custom-call(s32[4]{0:T(128)S(1)} %bitcast_select_fusion.1.which_ref, f32[32,768]{1,0:T(8,128)S(1)} %shard_map.73.refs_0_, f32[32,768]{1,0:T(8,128)S(1)} %collective-permute-done.45.refs_1_, f32[32,768]{1,0:T(8,128)S(1)} %collective-permute-done.46.refs_2_, f32[32,768]{1,0:T(8,128)S(1)} %collective-permute-done.47.refs_3_, ...), custom_call_target="tpu_custom_call" | custom-call | tf_op jit(solution)/shard_map/pallas_call | solution.py:167
  139.6 2.6 %collective-permute-start.67 = (f32[32,768]{1,0:T(8,128)S(1)}, f32[32,768]{1,0:T(8,128)S(1)}, u32[]{:S(2)}, u32[]{:S(2)}) collective-permute-start(f32[32,768]{1,0:T(8,128)S(1)} %shard_map.74.refs_0_), channel_id=1, source_target_pairs={{0,8},{1,9},{2,10},{3,11},{4,12},{5,13},{6,14},{7,15},{8,0},{9,1},... | collective-permute-start | bytes 294920 | tf_op jit(solution)/shard_map/ppermute | solution.py:152
  144.4 2.4 %collective-permute-done.63.refs_4_ = f32[32,768]{1,0:T(8,128)S(1)} collective-permute-done((f32[32,768]{1,0:T(8,128)S(1)}, f32[32,768]{1,0:T(8,128)S(1)}, u32[]{:S(2)}, u32[]{:S(2)}) %collective-permute-start.63) | collective-permute-done | bytes 98336 | tf_op jit(solution)/shard_map/ppermute | solution.py:152
  148.1 2.1 collective-permute-done.67.refs_8_
  152.9 2.0 collective-permute-done.69.refs_10_
  158.0 11.1 %shard_map.75.refs_0_ = f32[32,768]{1,0:T(8,128)S(1)} custom-call(s32[4]{0:T(128)S(1)} %bitcast_select_fusion.1.which_ref, f32[32,768]{1,0:T(8,128)S(1)} %shard_map.74.refs_0_, f32[32,768]{1,0:T(8,128)S(1)} %collective-permute-done.60.refs_1_, f32[32,768]{1,0:T(8,128)S(1)} %collective-permute-done.61.refs_2_, f32[32,768]{1,0:T(8,128)S(1)} %collective-permute-done.62.refs_3_, ...), custom_call_target="tpu_custom_call" | custom-call | tf_op jit(solution)/shard_map/pallas_call | solution.py:167
  169.6 3.5 %collective-permute-start.82 = (f32[32,768]{1,0:T(8,128)S(1)}, f32[32,768]{1,0:T(8,128)S(1)}, u32[]{:S(2)}, u32[]{:S(2)}) collective-permute-start(f32[32,768]{1,0:T(8,128)S(1)} %shard_map.75.refs_0_), channel_id=1, source_target_pairs={{0,8},{1,9},{2,10},{3,11},{4,12},{5,13},{6,14},{7,15},{8,0},{9,1},... | collective-permute-start | bytes 294920 | tf_op jit(solution)/shard_map/ppermute | solution.py:152
  173.9 2.7 %collective-permute-done.78.refs_4_ = f32[32,768]{1,0:T(8,128)S(1)} collective-permute-done((f32[32,768]{1,0:T(8,128)S(1)}, f32[32,768]{1,0:T(8,128)S(1)}, u32[]{:S(2)}, u32[]{:S(2)}) %collective-permute-start.78) | collective-permute-done | bytes 98336 | tf_op jit(solution)/shard_map/ppermute | solution.py:152
  177.6 2.4 collective-permute-done.82.refs_8_
  182.7 3.0 %collective-permute-done.84.refs_10_ = f32[32,768]{1,0:T(8,128)S(1)} collective-permute-done((f32[32,768]{1,0:T(8,128)S(1)}, f32[32,768]{1,0:T(8,128)S(1)}, u32[]{:S(2)}, u32[]{:S(2)}) %collective-permute-start.84) | collective-permute-done | bytes 98336 | tf_op jit(solution)/shard_map/ppermute | solution.py:152
  188.7 3.7 %copy-done.1 = bf16[8,768,768]{2,1,0:T(8,128)(2,1)S(1)} copy-done((bf16[8,768,768]{2,1,0:T(8,128)(2,1)S(1)}, bf16[8,768,768]{2,1,0:T(8,128)(2,1)}, u32[]{:S(2)}) %copy-start.1) | copy-done | bytes 9437208
  192.4 3.7 %copy-done.3 = bf16[8,768,768]{2,1,0:T(8,128)(2,1)S(1)} copy-done((bf16[8,768,768]{2,1,0:T(8,128)(2,1)S(1)}, bf16[8,768,768]{2,1,0:T(8,128)(2,1)}, u32[]{:S(2)}) %copy-start.3) | copy-done | bytes 9437208
  196.1 1.7 copy-done.6
  197.8 11.3 %shard_map.76 = f32[32,768]{1,0:T(8,128)} custom-call(s32[4]{0:T(128)S(1)} %bitcast_select_fusion.1.which_ref, f32[32,768]{1,0:T(8,128)S(1)} %shard_map.75.refs_0_, f32[32,768]{1,0:T(8,128)S(1)} %collective-permute-done.75.refs_1_, f32[32,768]{1,0:T(8,128)S(1)} %collective-permute-done.76.refs_2_, f32[32,768]{1,0:T(8,128)S(1)} %collective-permute-done.77.refs_3_, ...), custom_call_target="tpu_custom_call" | custom-call | tf_op jit(solution)/shard_map/pallas_call | solution.py:167
  210.2 32.3 %psum.7 = f32[1,2,16]{2,1,0:T(2,128)} all-reduce(f32[1,2,16]{2,1,0:T(2,128)S(1)} %broadcast_in_dim.5), channel_id=1, replica_groups=mesh['farm'=2,'body'=16] {'body'}, use_global_device_ids=true, to_apply=%region_1.2 | all-reduce | flops 32 | bytes 256 | tf_op jit(solution)/shard_map/psum | solution.py:171
  (172 shorter events, 43.4 us)
Async XLA Ops:
  7.5 10.4 %collective-permute-start.7 = (f32[32,768]{1,0:T(8,128)S(1)}, f32[32,768]{1,0:T(8,128)S(1)}, u32[]{:S(2)}, u32[]{:S(2)}) collective-permute-start(f32[32,768]{1,0:T(8,128)S(1)} %shard_map.69.refs_0_), channel_id=1, source_target_pairs={{0,8},{1,9},{2,10},{3,11},{4,12},{5,13},{6,14},{7,15},{8,0},{9,1},... | collective-permute-start | bytes 294920 | tf_op jit(solution)/shard_map/ppermute | solution.py:152
  11.6 8.1 %collective-permute-start.11 = (f32[32,768]{1,0:T(8,128)S(1)}, f32[32,768]{1,0:T(8,128)S(1)}, u32[]{:S(2)}, u32[]{:S(2)}) collective-permute-start(f32[32,768]{1,0:T(8,128)S(1)} %shard_map.69.refs_0_), channel_id=1, source_target_pairs={{0,12},{1,13},{2,14},{3,15},{4,0},{5,1},{6,2},{7,3},{8,4},{9,5},{1... | collective-permute-start | bytes 294920 | tf_op jit(solution)/shard_map/ppermute | solution.py:152
  12.9 7.0 %collective-permute-start.3 = (f32[32,768]{1,0:T(8,128)S(1)}, f32[32,768]{1,0:T(8,128)S(1)}, u32[]{:S(2)}, u32[]{:S(2)}) collective-permute-start(f32[32,768]{1,0:T(8,128)S(1)} %shard_map.69.refs_0_), channel_id=1, source_target_pairs={{0,4},{1,5},{2,6},{3,7},{4,8},{5,9},{6,10},{7,11},{8,12},{9,13},{1... | collective-permute-start | bytes 294920 | tf_op jit(solution)/shard_map/ppermute | solution.py:152
  13.6 8.1 %collective-permute-start.1 = (f32[32,768]{1,0:T(8,128)S(1)}, f32[32,768]{1,0:T(8,128)S(1)}, u32[]{:S(2)}, u32[]{:S(2)}) collective-permute-start(f32[32,768]{1,0:T(8,128)S(1)} %shard_map.69.refs_0_), channel_id=1, source_target_pairs={{0,2},{1,3},{2,0},{3,1},{4,6},{5,7},{6,4},{7,5},{8,10},{9,11},{10,... | collective-permute-start | bytes 294920 | tf_op jit(solution)/shard_map/ppermute | solution.py:152
  15.1 6.6 %collective-permute-start = (f32[32,768]{1,0:T(8,128)S(1)}, f32[32,768]{1,0:T(8,128)S(1)}, u32[]{:S(2)}, u32[]{:S(2)}) collective-permute-start(f32[32,768]{1,0:T(8,128)S(1)} %shard_map.69.refs_0_), channel_id=1, source_target_pairs={{0,1},{1,0},{2,3},{3,2},{4,5},{5,4},{6,7},{7,6},{8,9},{9,8},{10,11... | collective-permute-start | bytes 294920 | tf_op jit(solution)/shard_map/ppermute | solution.py:152
  17.9 5.7 %collective-permute-start.9 = (f32[32,768]{1,0:T(8,128)S(1)}, f32[32,768]{1,0:T(8,128)S(1)}, u32[]{:S(2)}, u32[]{:S(2)}) collective-permute-start(f32[32,768]{1,0:T(8,128)S(1)} %collective-permute-done.7.refs_8_), channel_id=1, source_target_pairs={{0,2},{1,3},{2,0},{3,1},{4,6},{5,7},{6,4},{7,5},{8,10},{9,11},{10,... | collective-permute-start | bytes 294920 | tf_op jit(solution)/shard_map/ppermute | solution.py:152
  19.9 5.7 %collective-permute-start.5 = (f32[32,768]{1,0:T(8,128)S(1)}, f32[32,768]{1,0:T(8,128)S(1)}, u32[]{:S(2)}, u32[]{:S(2)}) collective-permute-start(f32[32,768]{1,0:T(8,128)S(1)} %collective-permute-done.3.refs_4_), channel_id=1, source_target_pairs={{0,2},{1,3},{2,0},{3,1},{4,6},{5,7},{6,4},{7,5},{8,10},{9,11},{10,... | collective-permute-start | bytes 294920 | tf_op jit(solution)/shard_map/ppermute | solution.py:152
  23.6 12.0 %collective-permute-start.8 = (f32[32,768]{1,0:T(8,128)S(1)}, f32[32,768]{1,0:T(8,128)S(1)}, u32[]{:S(2)}, u32[]{:S(2)}) collective-permute-start(f32[32,768]{1,0:T(8,128)S(1)} %collective-permute-done.7.refs_8_), channel_id=1, source_target_pairs={{0,1},{1,0},{2,3},{3,2},{4,5},{5,4},{6,7},{7,6},{8,9},{9,8},{10,11... | collective-permute-start | bytes 294920 | tf_op jit(solution)/shard_map/ppermute | solution.py:152
  24.6 10.9 %collective-permute-start.2 = (f32[32,768]{1,0:T(8,128)S(1)}, f32[32,768]{1,0:T(8,128)S(1)}, u32[]{:S(2)}, u32[]{:S(2)}) collective-permute-start(f32[32,768]{1,0:T(8,128)S(1)} %collective-permute-done.1.refs_2_), channel_id=1, source_target_pairs={{0,1},{1,0},{2,3},{3,2},{4,5},{5,4},{6,7},{7,6},{8,9},{9,8},{10,11... | collective-permute-start | bytes 294920 | tf_op jit(solution)/shard_map/ppermute | solution.py:152
  25.7 9.9 %collective-permute-start.10 = (f32[32,768]{1,0:T(8,128)S(1)}, f32[32,768]{1,0:T(8,128)S(1)}, u32[]{:S(2)}, u32[]{:S(2)}) collective-permute-start(f32[32,768]{1,0:T(8,128)S(1)} %collective-permute-done.9.refs_10_), channel_id=1, source_target_pairs={{0,1},{1,0},{2,3},{3,2},{4,5},{5,4},{6,7},{7,6},{8,9},{9,8},{10,11... | collective-permute-start | bytes 294920 | tf_op jit(solution)/shard_map/ppermute | solution.py:152
  25.7 9.9 %collective-permute-start.14 = (f32[32,768]{1,0:T(8,128)S(1)}, f32[32,768]{1,0:T(8,128)S(1)}, u32[]{:S(2)}, u32[]{:S(2)}) collective-permute-start(f32[32,768]{1,0:T(8,128)S(1)} %collective-permute-done.13.refs_14_), channel_id=1, source_target_pairs={{0,1},{1,0},{2,3},{3,2},{4,5},{5,4},{6,7},{7,6},{8,9},{9,8},{10,11... | collective-permute-start | bytes 294920 | tf_op jit(solution)/shard_map/ppermute | solution.py:152
  26.2 9.4 %collective-permute-start.6 = (f32[32,768]{1,0:T(8,128)S(1)}, f32[32,768]{1,0:T(8,128)S(1)}, u32[]{:S(2)}, u32[]{:S(2)}) collective-permute-start(f32[32,768]{1,0:T(8,128)S(1)} %collective-permute-done.5.refs_6_), channel_id=1, source_target_pairs={{0,1},{1,0},{2,3},{3,2},{4,5},{5,4},{6,7},{7,6},{8,9},{9,8},{10,11... | collective-permute-start | bytes 294920 | tf_op jit(solution)/shard_map/ppermute | solution.py:152
  46.4 9.2 %collective-permute-start.18 = (f32[32,768]{1,0:T(8,128)S(1)}, f32[32,768]{1,0:T(8,128)S(1)}, u32[]{:S(2)}, u32[]{:S(2)}) collective-permute-start(f32[32,768]{1,0:T(8,128)S(1)} %shard_map.71.refs_0_), channel_id=1, source_target_pairs={{0,4},{1,5},{2,6},{3,7},{4,8},{5,9},{6,10},{7,11},{8,12},{9,13},{1... | collective-permute-start | bytes 294920 | tf_op jit(solution)/shard_map/ppermute | solution.py:152
  49.0 10.5 %collective-permute-start.22 = (f32[32,768]{1,0:T(8,128)S(1)}, f32[32,768]{1,0:T(8,128)S(1)}, u32[]{:S(2)}, u32[]{:S(2)}) collective-permute-start(f32[32,768]{1,0:T(8,128)S(1)} %shard_map.71.refs_0_), channel_id=1, source_target_pairs={{0,8},{1,9},{2,10},{3,11},{4,12},{5,13},{6,14},{7,15},{8,0},{9,1},... | collective-permute-start | bytes 294920 | tf_op jit(solution)/shard_map/ppermute | solution.py:152
  52.5 8.6 %collective-permute-start.26 = (f32[32,768]{1,0:T(8,128)S(1)}, f32[32,768]{1,0:T(8,128)S(1)}, u32[]{:S(2)}, u32[]{:S(2)}) collective-permute-start(f32[32,768]{1,0:T(8,128)S(1)} %shard_map.71.refs_0_), channel_id=1, source_target_pairs={{0,12},{1,13},{2,14},{3,15},{4,0},{5,1},{6,2},{7,3},{8,4},{9,5},{1... | collective-permute-start | bytes 294920 | tf_op jit(solution)/shard_map/ppermute | solution.py:152
  52.5 9.0 %collective-permute-start.16 = (f32[32,768]{1,0:T(8,128)S(1)}, f32[32,768]{1,0:T(8,128)S(1)}, u32[]{:S(2)}, u32[]{:S(2)}) collective-permute-start(f32[32,768]{1,0:T(8,128)S(1)} %shard_map.71.refs_0_), channel_id=1, source_target_pairs={{0,2},{1,3},{2,0},{3,1},{4,6},{5,7},{6,4},{7,5},{8,10},{9,11},{10,... | collective-permute-start | bytes 294920 | tf_op jit(solution)/shard_map/ppermute | solution.py:152
  53.9 7.6 %collective-permute-start.15 = (f32[32,768]{1,0:T(8,128)S(1)}, f32[32,768]{1,0:T(8,128)S(1)}, u32[]{:S(2)}, u32[]{:S(2)}) collective-permute-start(f32[32,768]{1,0:T(8,128)S(1)} %shard_map.71.refs_0_), channel_id=1, source_target_pairs={{0,1},{1,0},{2,3},{3,2},{4,5},{5,4},{6,7},{7,6},{8,9},{9,8},{10,11... | collective-permute-start | bytes 294920 | tf_op jit(solution)/shard_map/ppermute | solution.py:152
  55.6 6.4 %collective-permute-start.20 = (f32[32,768]{1,0:T(8,128)S(1)}, f32[32,768]{1,0:T(8,128)S(1)}, u32[]{:S(2)}, u32[]{:S(2)}) collective-permute-start(f32[32,768]{1,0:T(8,128)S(1)} %collective-permute-done.18.refs_4_), channel_id=1, source_target_pairs={{0,2},{1,3},{2,0},{3,1},{4,6},{5,7},{6,4},{7,5},{8,10},{9,11},{10,... | collective-permute-start | bytes 294920 | tf_op jit(solution)/shard_map/ppermute | solution.py:152
  59.5 5.5 %collective-permute-start.24 = (f32[32,768]{1,0:T(8,128)S(1)}, f32[32,768]{1,0:T(8,128)S(1)}, u32[]{:S(2)}, u32[]{:S(2)}) collective-permute-start(f32[32,768]{1,0:T(8,128)S(1)} %collective-permute-done.22.refs_8_), channel_id=1, source_target_pairs={{0,2},{1,3},{2,0},{3,1},{4,6},{5,7},{6,4},{7,5},{8,10},{9,11},{10,... | collective-permute-start | bytes 294920 | tf_op jit(solution)/shard_map/ppermute | solution.py:152
  61.5 5.3 %collective-permute-start.19 = (f32[32,768]{1,0:T(8,128)S(1)}, f32[32,768]{1,0:T(8,128)S(1)}, u32[]{:S(2)}, u32[]{:S(2)}) collective-permute-start(f32[32,768]{1,0:T(8,128)S(1)} %collective-permute-done.18.refs_4_), channel_id=1, source_target_pairs={{0,1},{1,0},{2,3},{3,2},{4,5},{5,4},{6,7},{7,6},{8,9},{9,8},{10,11... | collective-permute-start | bytes 294920 | tf_op jit(solution)/shard_map/ppermute | solution.py:152
  79.0 7.8 %collective-permute-start.33 = (f32[32,768]{1,0:T(8,128)S(1)}, f32[32,768]{1,0:T(8,128)S(1)}, u32[]{:S(2)}, u32[]{:S(2)}) collective-permute-start(f32[32,768]{1,0:T(8,128)S(1)} %shard_map.72.refs_0_), channel_id=1, source_target_pairs={{0,4},{1,5},{2,6},{3,7},{4,8},{5,9},{6,10},{7,11},{8,12},{9,13},{1... | collective-permute-start | bytes 294920 | tf_op jit(solution)/shard_map/ppermute | solution.py:152
  79.7 10.5 %collective-permute-start.37 = (f32[32,768]{1,0:T(8,128)S(1)}, f32[32,768]{1,0:T(8,128)S(1)}, u32[]{:S(2)}, u32[]{:S(2)}) collective-permute-start(f32[32,768]{1,0:T(8,128)S(1)} %shard_map.72.refs_0_), channel_id=1, source_target_pairs={{0,8},{1,9},{2,10},{3,11},{4,12},{5,13},{6,14},{7,15},{8,0},{9,1},... | collective-permute-start | bytes 294920 | tf_op jit(solution)/shard_map/ppermute | solution.py:152
  82.5 9.3 %collective-permute-start.41 = (f32[32,768]{1,0:T(8,128)S(1)}, f32[32,768]{1,0:T(8,128)S(1)}, u32[]{:S(2)}, u32[]{:S(2)}) collective-permute-start(f32[32,768]{1,0:T(8,128)S(1)} %shard_map.72.refs_0_), channel_id=1, source_target_pairs={{0,12},{1,13},{2,14},{3,15},{4,0},{5,1},{6,2},{7,3},{8,4},{9,5},{1... | collective-permute-start | bytes 294920 | tf_op jit(solution)/shard_map/ppermute | solution.py:152
  83.0 9.2 %collective-permute-start.31 = (f32[32,768]{1,0:T(8,128)S(1)}, f32[32,768]{1,0:T(8,128)S(1)}, u32[]{:S(2)}, u32[]{:S(2)}) collective-permute-start(f32[32,768]{1,0:T(8,128)S(1)} %shard_map.72.refs_0_), channel_id=1, source_target_pairs={{0,2},{1,3},{2,0},{3,1},{4,6},{5,7},{6,4},{7,5},{8,10},{9,11},{10,... | collective-permute-start | bytes 294920 | tf_op jit(solution)/shard_map/ppermute | solution.py:152
  84.7 7.5 %collective-permute-start.30 = (f32[32,768]{1,0:T(8,128)S(1)}, f32[32,768]{1,0:T(8,128)S(1)}, u32[]{:S(2)}, u32[]{:S(2)}) collective-permute-start(f32[32,768]{1,0:T(8,128)S(1)} %shard_map.72.refs_0_), channel_id=1, source_target_pairs={{0,1},{1,0},{2,3},{3,2},{4,5},{5,4},{6,7},{7,6},{8,9},{9,8},{10,11... | collective-permute-start | bytes 294920 | tf_op jit(solution)/shard_map/ppermute | solution.py:152
  86.7 6.0 %collective-permute-start.35 = (f32[32,768]{1,0:T(8,128)S(1)}, f32[32,768]{1,0:T(8,128)S(1)}, u32[]{:S(2)}, u32[]{:S(2)}) collective-permute-start(f32[32,768]{1,0:T(8,128)S(1)} %collective-permute-done.33.refs_4_), channel_id=1, source_target_pairs={{0,2},{1,3},{2,0},{3,1},{4,6},{5,7},{6,4},{7,5},{8,10},{9,11},{10,... | collective-permute-start | bytes 294920 | tf_op jit(solution)/shard_map/ppermute | solution.py:152
  109.1 7.6 %collective-permute-start.48 = (f32[32,768]{1,0:T(8,128)S(1)}, f32[32,768]{1,0:T(8,128)S(1)}, u32[]{:S(2)}, u32[]{:S(2)}) collective-permute-start(f32[32,768]{1,0:T(8,128)S(1)} %shard_map.73.refs_0_), channel_id=1, source_target_pairs={{0,4},{1,5},{2,6},{3,7},{4,8},{5,9},{6,10},{7,11},{8,12},{9,13},{1... | collective-permute-start | bytes 294920 | tf_op jit(solution)/shard_map/ppermute | solution.py:152
  109.3 10.8 %collective-permute-start.52 = (f32[32,768]{1,0:T(8,128)S(1)}, f32[32,768]{1,0:T(8,128)S(1)}, u32[]{:S(2)}, u32[]{:S(2)}) collective-permute-start(f32[32,768]{1,0:T(8,128)S(1)} %shard_map.73.refs_0_), channel_id=1, source_target_pairs={{0,8},{1,9},{2,10},{3,11},{4,12},{5,13},{6,14},{7,15},{8,0},{9,1},... | collective-permute-start | bytes 294920 | tf_op jit(solution)/shard_map/ppermute | solution.py:152
  112.8 8.3 %collective-permute-start.56 = (f32[32,768]{1,0:T(8,128)S(1)}, f32[32,768]{1,0:T(8,128)S(1)}, u32[]{:S(2)}, u32[]{:S(2)}) collective-permute-start(f32[32,768]{1,0:T(8,128)S(1)} %shard_map.73.refs_0_), channel_id=1, source_target_pairs={{0,12},{1,13},{2,14},{3,15},{4,0},{5,1},{6,2},{7,3},{8,4},{9,5},{1... | collective-permute-start | bytes 294920 | tf_op jit(solution)/shard_map/ppermute | solution.py:152
  113.0 9.1 %collective-permute-start.46 = (f32[32,768]{1,0:T(8,128)S(1)}, f32[32,768]{1,0:T(8,128)S(1)}, u32[]{:S(2)}, u32[]{:S(2)}) collective-permute-start(f32[32,768]{1,0:T(8,128)S(1)} %shard_map.73.refs_0_), channel_id=1, source_target_pairs={{0,2},{1,3},{2,0},{3,1},{4,6},{5,7},{6,4},{7,5},{8,10},{9,11},{10,... | collective-permute-start | bytes 294920 | tf_op jit(solution)/shard_map/ppermute | solution.py:152
  114.1 8.0 %collective-permute-start.45 = (f32[32,768]{1,0:T(8,128)S(1)}, f32[32,768]{1,0:T(8,128)S(1)}, u32[]{:S(2)}, u32[]{:S(2)}) collective-permute-start(f32[32,768]{1,0:T(8,128)S(1)} %shard_map.73.refs_0_), channel_id=1, source_target_pairs={{0,1},{1,0},{2,3},{3,2},{4,5},{5,4},{6,7},{7,6},{8,9},{9,8},{10,11... | collective-permute-start | bytes 294920 | tf_op jit(solution)/shard_map/ppermute | solution.py:152
  116.7 5.9 %collective-permute-start.50 = (f32[32,768]{1,0:T(8,128)S(1)}, f32[32,768]{1,0:T(8,128)S(1)}, u32[]{:S(2)}, u32[]{:S(2)}) collective-permute-start(f32[32,768]{1,0:T(8,128)S(1)} %collective-permute-done.48.refs_4_), channel_id=1, source_target_pairs={{0,2},{1,3},{2,0},{3,1},{4,6},{5,7},{6,4},{7,5},{8,10},{9,11},{10,... | collective-permute-start | bytes 294920 | tf_op jit(solution)/shard_map/ppermute | solution.py:152
  120.1 5.4 %collective-permute-start.54 = (f32[32,768]{1,0:T(8,128)S(1)}, f32[32,768]{1,0:T(8,128)S(1)}, u32[]{:S(2)}, u32[]{:S(2)}) collective-permute-start(f32[32,768]{1,0:T(8,128)S(1)} %collective-permute-done.52.refs_8_), channel_id=1, source_target_pairs={{0,2},{1,3},{2,0},{3,1},{4,6},{5,7},{6,4},{7,5},{8,10},{9,11},{10,... | collective-permute-start | bytes 294920 | tf_op jit(solution)/shard_map/ppermute | solution.py:152
  121.1 5.5 %collective-permute-start.58 = (f32[32,768]{1,0:T(8,128)S(1)}, f32[32,768]{1,0:T(8,128)S(1)}, u32[]{:S(2)}, u32[]{:S(2)}) collective-permute-start(f32[32,768]{1,0:T(8,128)S(1)} %collective-permute-done.56.refs_12_), channel_id=1, source_target_pairs={{0,2},{1,3},{2,0},{3,1},{4,6},{5,7},{6,4},{7,5},{8,10},{9,11},{10,... | collective-permute-start | bytes 294920 | tf_op jit(solution)/shard_map/ppermute | solution.py:152
  139.2 7.6 %collective-permute-start.63 = (f32[32,768]{1,0:T(8,128)S(1)}, f32[32,768]{1,0:T(8,128)S(1)}, u32[]{:S(2)}, u32[]{:S(2)}) collective-permute-start(f32[32,768]{1,0:T(8,128)S(1)} %shard_map.74.refs_0_), channel_id=1, source_target_pairs={{0,4},{1,5},{2,6},{3,7},{4,8},{5,9},{6,10},{7,11},{8,12},{9,13},{1... | collective-permute-start | bytes 294920 | tf_op jit(solution)/shard_map/ppermute | solution.py:152
  139.6 10.6 %collective-permute-start.67 = (f32[32,768]{1,0:T(8,128)S(1)}, f32[32,768]{1,0:T(8,128)S(1)}, u32[]{:S(2)}, u32[]{:S(2)}) collective-permute-start(f32[32,768]{1,0:T(8,128)S(1)} %shard_map.74.refs_0_), channel_id=1, source_target_pairs={{0,8},{1,9},{2,10},{3,11},{4,12},{5,13},{6,14},{7,15},{8,0},{9,1},... | collective-permute-start | bytes 294920 | tf_op jit(solution)/shard_map/ppermute | solution.py:152
  142.2 9.3 %collective-permute-start.71 = (f32[32,768]{1,0:T(8,128)S(1)}, f32[32,768]{1,0:T(8,128)S(1)}, u32[]{:S(2)}, u32[]{:S(2)}) collective-permute-start(f32[32,768]{1,0:T(8,128)S(1)} %shard_map.74.refs_0_), channel_id=1, source_target_pairs={{0,12},{1,13},{2,14},{3,15},{4,0},{5,1},{6,2},{7,3},{8,4},{9,5},{1... | collective-permute-start | bytes 294920 | tf_op jit(solution)/shard_map/ppermute | solution.py:152
  143.1 9.2 %collective-permute-start.61 = (f32[32,768]{1,0:T(8,128)S(1)}, f32[32,768]{1,0:T(8,128)S(1)}, u32[]{:S(2)}, u32[]{:S(2)}) collective-permute-start(f32[32,768]{1,0:T(8,128)S(1)} %shard_map.74.refs_0_), channel_id=1, source_target_pairs={{0,2},{1,3},{2,0},{3,1},{4,6},{5,7},{6,4},{7,5},{8,10},{9,11},{10,... | collective-permute-start | bytes 294920 | tf_op jit(solution)/shard_map/ppermute | solution.py:152
  144.4 7.9 %collective-permute-start.60 = (f32[32,768]{1,0:T(8,128)S(1)}, f32[32,768]{1,0:T(8,128)S(1)}, u32[]{:S(2)}, u32[]{:S(2)}) collective-permute-start(f32[32,768]{1,0:T(8,128)S(1)} %shard_map.74.refs_0_), channel_id=1, source_target_pairs={{0,1},{1,0},{2,3},{3,2},{4,5},{5,4},{6,7},{7,6},{8,9},{9,8},{10,11... | collective-permute-start | bytes 294920 | tf_op jit(solution)/shard_map/ppermute | solution.py:152
  146.8 6.0 %collective-permute-start.65 = (f32[32,768]{1,0:T(8,128)S(1)}, f32[32,768]{1,0:T(8,128)S(1)}, u32[]{:S(2)}, u32[]{:S(2)}) collective-permute-start(f32[32,768]{1,0:T(8,128)S(1)} %collective-permute-done.63.refs_4_), channel_id=1, source_target_pairs={{0,2},{1,3},{2,0},{3,1},{4,6},{5,7},{6,4},{7,5},{8,10},{9,11},{10,... | collective-permute-start | bytes 294920 | tf_op jit(solution)/shard_map/ppermute | solution.py:152
  169.1 7.6 %collective-permute-start.78 = (f32[32,768]{1,0:T(8,128)S(1)}, f32[32,768]{1,0:T(8,128)S(1)}, u32[]{:S(2)}, u32[]{:S(2)}) collective-permute-start(f32[32,768]{1,0:T(8,128)S(1)} %shard_map.75.refs_0_), channel_id=1, source_target_pairs={{0,4},{1,5},{2,6},{3,7},{4,8},{5,9},{6,10},{7,11},{8,12},{9,13},{1... | collective-permute-start | bytes 294920 | tf_op jit(solution)/shard_map/ppermute | solution.py:152
  169.6 10.5 %collective-permute-start.82 = (f32[32,768]{1,0:T(8,128)S(1)}, f32[32,768]{1,0:T(8,128)S(1)}, u32[]{:S(2)}, u32[]{:S(2)}) collective-permute-start(f32[32,768]{1,0:T(8,128)S(1)} %shard_map.75.refs_0_), channel_id=1, source_target_pairs={{0,8},{1,9},{2,10},{3,11},{4,12},{5,13},{6,14},{7,15},{8,0},{9,1},... | collective-permute-start | bytes 294920 | tf_op jit(solution)/shard_map/ppermute | solution.py:152
  173.1 7.9 %collective-permute-start.86 = (f32[32,768]{1,0:T(8,128)S(1)}, f32[32,768]{1,0:T(8,128)S(1)}, u32[]{:S(2)}, u32[]{:S(2)}) collective-permute-start(f32[32,768]{1,0:T(8,128)S(1)} %shard_map.75.refs_0_), channel_id=1, source_target_pairs={{0,12},{1,13},{2,14},{3,15},{4,0},{5,1},{6,2},{7,3},{8,4},{9,5},{1... | collective-permute-start | bytes 294920 | tf_op jit(solution)/shard_map/ppermute | solution.py:152
  173.1 9.0 %collective-permute-start.76 = (f32[32,768]{1,0:T(8,128)S(1)}, f32[32,768]{1,0:T(8,128)S(1)}, u32[]{:S(2)}, u32[]{:S(2)}) collective-permute-start(f32[32,768]{1,0:T(8,128)S(1)} %shard_map.75.refs_0_), channel_id=1, source_target_pairs={{0,2},{1,3},{2,0},{3,1},{4,6},{5,7},{6,4},{7,5},{8,10},{9,11},{10,... | collective-permute-start | bytes 294920 | tf_op jit(solution)/shard_map/ppermute | solution.py:152
  173.9 8.2 %collective-permute-start.75 = (f32[32,768]{1,0:T(8,128)S(1)}, f32[32,768]{1,0:T(8,128)S(1)}, u32[]{:S(2)}, u32[]{:S(2)}) collective-permute-start(f32[32,768]{1,0:T(8,128)S(1)} %shard_map.75.refs_0_), channel_id=1, source_target_pairs={{0,1},{1,0},{2,3},{3,2},{4,5},{5,4},{6,7},{7,6},{8,9},{9,8},{10,11... | collective-permute-start | bytes 294920 | tf_op jit(solution)/shard_map/ppermute | solution.py:152
  176.6 6.0 %collective-permute-start.80 = (f32[32,768]{1,0:T(8,128)S(1)}, f32[32,768]{1,0:T(8,128)S(1)}, u32[]{:S(2)}, u32[]{:S(2)}) collective-permute-start(f32[32,768]{1,0:T(8,128)S(1)} %collective-permute-done.78.refs_4_), channel_id=1, source_target_pairs={{0,2},{1,3},{2,0},{3,1},{4,6},{5,7},{6,4},{7,5},{8,10},{9,11},{10,... | collective-permute-start | bytes 294920 | tf_op jit(solution)/shard_map/ppermute | solution.py:152
  180.1 5.7 %collective-permute-start.84 = (f32[32,768]{1,0:T(8,128)S(1)}, f32[32,768]{1,0:T(8,128)S(1)}, u32[]{:S(2)}, u32[]{:S(2)}) collective-permute-start(f32[32,768]{1,0:T(8,128)S(1)} %collective-permute-done.82.refs_8_), channel_id=1, source_target_pairs={{0,2},{1,3},{2,0},{3,1},{4,6},{5,7},{6,4},{7,5},{8,10},{9,11},{10,... | collective-permute-start | bytes 294920 | tf_op jit(solution)/shard_map/ppermute | solution.py:152
  181.0 5.8 %collective-permute-start.88 = (f32[32,768]{1,0:T(8,128)S(1)}, f32[32,768]{1,0:T(8,128)S(1)}, u32[]{:S(2)}, u32[]{:S(2)}) collective-permute-start(f32[32,768]{1,0:T(8,128)S(1)} %collective-permute-done.86.refs_12_), channel_id=1, source_target_pairs={{0,2},{1,3},{2,0},{3,1},{4,6},{5,7},{6,4},{7,5},{8,10},{9,11},{10,... | collective-permute-start | bytes 294920 | tf_op jit(solution)/shard_map/ppermute | solution.py:152
  (55 other events, 475.8 us)
